TPU v7x, 32 devices: a whole 2x2x4 slice. The times are simulated.
32 devices in a mesh: stn: 2 (over y), tm: 8 (over z, core), cores: 2 (over x).
Axes of the slice: x: 2, y: 2, z: 4, core: 2. Of those that a mesh axis runs over, the one named last changes fastest.
Arguments:
- samples: bfloat16 [64, 2097152], P('stn', ('tm', 'cores')), may hold values from -6 to 6
- delays: int32 [64], P('stn'), may hold values from 0 to 32768, as said below
- valid: int32 [64], P('stn'), may hold values 0 or 1
- tone_chan: int32 [64, 64], P('stn'), may hold values from 0 to 16383
Outputs:
- visibility: float32 [16384, 8192], P(('stn', 'tm', 'cores'))
- phase_cal: float32 [64, 128], P('stn')
Inputs may be any that keep to these rules, and one draw needn't show every extreme that they name: `delays`: each station's delay in samples; some station has a delay of exactly 32768.
All inputs are finite; a program needn't handle non-finite values. No bound on the sum of `valid` on one device may be relied on, other than what follows from the above.
Results may differ from a plain program's by a relative error of at most 0.007.
Values may be sent and summed in bfloat16 or wider, within the bound.
A program may use at most 128 MiB of HBM per device.

v0:
```python
import math

import jax
import jax.numpy as jnp
from jax import lax
from jax.sharding import PartitionSpec as P

S = 64
NCH = 16384
FA = 256
FB = 128
NTONE = 64
MAXD = 32768


def passed_along(block, axis, distance):
    devices = range(lax.axis_size(axis))
    route = [(i - distance, i) for i in devices if i - distance in devices]
    return lax.ppermute(block, axis, route)


def make_tables():
    outer_idx = jnp.arange(FA, dtype=jnp.int32)
    phases = outer_idx[:, None] * outer_idx[None, :] % FA
    angles = 2.0 * math.pi / FA * phases.astype(jnp.float32)
    section_one = jnp.stack([jnp.cos(angles), -jnp.sin(angles)]).astype(jnp.bfloat16)
    inner_idx = jnp.arange(FB, dtype=jnp.int32)
    spectrum_len = FA * FB
    twist_idx = outer_idx[:, None] * inner_idx[None, :] % spectrum_len
    twists = 2.0 * math.pi / spectrum_len * twist_idx.astype(jnp.float32)
    norm_scale = 1.0 / math.sqrt(spectrum_len)
    twist_cos = jnp.cos(twists) * norm_scale
    twist_sin = jnp.sin(twists) * norm_scale
    half_idx = jnp.arange(FB // 2, dtype=jnp.int32)
    last_idx = inner_idx[:, None] * half_idx[None, :] % FB
    thetas = 2.0 * math.pi / FB * last_idx.astype(jnp.float32)
    cosine = jnp.cos(thetas)
    sine_val = jnp.sin(thetas)
    section_two = jnp.stack(
        [jnp.stack([cosine, -sine_val], axis=1), jnp.stack([sine_val, cosine], axis=1)]
    ).astype(jnp.bfloat16)
    return (section_one, twist_cos, twist_sin, section_two)


def channelize(window, usable, tables):
    section_one, twist_cos, twist_sin, section_two = tables
    spec_count = window.shape[0] // (FA * FB)
    blocks = window.reshape(spec_count, FA, FB)
    section_out = jnp.einsum(
        "xkn,bnm->bxkm", section_one, blocks, preferred_element_type=jnp.float32
    )
    real_part = section_out[:, 0] * twist_cos + section_out[:, 1] * twist_sin
    imag_part = section_out[:, 1] * twist_cos - section_out[:, 0] * twist_sin
    twisted = jnp.stack([real_part, imag_part], axis=1).astype(jnp.bfloat16)
    product = jnp.einsum(
        "xnrq,bxkn->brqk", section_two, twisted, preferred_element_type=jnp.float32
    )
    return (product.reshape(spec_count, 2, NCH) * usable).astype(jnp.bfloat16)


def cross_power(matrix):
    gram = jnp.einsum("cta,ctb->cab", matrix, matrix, preferred_element_type=jnp.float32)
    real_re = gram[:, :S, :S]
    imag_im = gram[:, S:, S:]
    imag_re = gram[:, S:, :S]
    real_im = gram[:, :S, S:]
    channels = gram.shape[0]
    first = (real_re + imag_im).reshape(channels, S * S)
    second = (imag_re - real_im).reshape(channels, S * S)
    return jnp.concatenate([first, second], axis=1)


def shards(samples, delays, valid, tone_chan):
    tables = make_tables()
    stretch = samples.shape[1]
    spectrum_len = FA * FB
    trailing = passed_along(samples[:, :MAXD], ("tm", "cores"), -1)
    extended = jnp.concatenate([samples, trailing], axis=1)
    chan_ids = jnp.arange(NCH, dtype=jnp.int32)

    def station(inputs):
        stream, shift_by, usable, tone_ids = inputs
        window = lax.dynamic_slice_in_dim(stream, shift_by, stretch)
        spectra = channelize(window, usable.astype(jnp.float32), tables)
        totals = jnp.sum(spectra, axis=0, dtype=jnp.float32)
        selector = (chan_ids[:, None] == tone_ids[None, :]).astype(jnp.float32)
        picked = jnp.dot(
            totals, selector, precision=lax.Precision.HIGHEST, preferred_element_type=jnp.float32
        )
        return (spectra, picked.reshape(2 * NTONE))

    spectra, tone_picks = lax.map(station, (extended, delays, valid, tone_chan))
    spectra_all = stretch // spectrum_len * lax.axis_size("tm") * lax.axis_size("cores")
    norm_scale = 1.0 / math.sqrt(spectra_all)
    phase_cal = lax.psum(tone_picks, ("tm", "cores")) * norm_scale
    local_stn = spectra.shape[0]
    spec_here = spectra.shape[1]
    n_stn = lax.axis_size("stn")
    n_tm = lax.axis_size("tm")
    received = lax.all_to_all(spectra[None], ("stn", "tm"), split_axis=4, concat_axis=0, tiled=True)
    block_in = received.shape[4]
    arranged = received.reshape(n_stn, n_tm, local_stn, spec_here, 2, block_in)
    turned = jnp.transpose(arranged, (0, 2, 1, 3, 4, 5)).reshape(
        n_stn * local_stn, n_tm * spec_here, 2, block_in
    )
    block = turned.shape[3]
    halves = turned.reshape(turned.shape[0], turned.shape[1], 2, 2, block // 2)
    halves = lax.all_to_all(halves, "cores", split_axis=3, concat_axis=1, tiled=True)
    turned = halves.reshape(halves.shape[0], halves.shape[1], 2, block // 2)
    rows = turned.shape[1]
    matrix = jnp.transpose(turned, (3, 1, 2, 0)).reshape(turned.shape[3], rows, 2 * S)
    partial_value = cross_power(matrix)
    return (partial_value * norm_scale, phase_cal)


def solution(mesh):
    return jax.shard_map(
        shards,
        mesh=mesh,
        in_specs=(P("stn", ("tm", "cores")), P("stn"), P("stn"), P("stn", None)),
        out_specs=(P(("stn", "tm", "cores"), None), P("stn", None)),
        check_vma=False,
    )
```

profile of v0, /device:TPU:0, one launch (start us, length us, event | category | flops | bytes accessed | tf_op | source)
XLA Modules:
  0.0 1132.0 jit_solution(16870476544510908703)
XLA Ops:
  6.5 47.9 %collective-permute-done = bf16[32,32768]{1,0:T(8,128)(2,1)S(1)} collective-permute-done((bf16[32,32768]{1,0:T(8,128)(2,1)}, bf16[32,32768]{1,0:T(8,128)(2,1)S(1)}, u32[]{:S(2)}, u32[]{:S(2)}) %collective-permute-start) | collective-permute-done | bytes 2097184 | tf_op jit(solution)/shard_map/ppermute | solution.py:19
  54.3 10.4 pad_maximum_fusion
  64.8 397.7 %while.17 = (s32[]{:T(128)}, bf16[32,4,2,16384]{3,2,1,0:T(2,128)(2,1)}, f32[32,128]{1,0:T(8,128)S(1)}, s32[32]{0:T(128)S(1)}, bf16[32,163840]{1,0:T(8,128)(2,1)}...) while((s32[]{:T(128)}, ...), condition=%wide.region_2.3_spmd.clone.clone, body=%wide.region_0.2_spmd.clone.clone.sunk | while | flops 230653952 | bytes 6622727 | solution.py:92
  69.1 3.5 dynamic-slice_reduce_fusion.2
  156.1 3.5 dynamic-slice_reduce_fusion.2
  168.5 3.5 dynamic-slice_reduce_fusion.2
  181.0 3.5 dynamic-slice_reduce_fusion.2
  193.4 3.5 dynamic-slice_reduce_fusion.2
  243.1 3.5 dynamic-slice_reduce_fusion.2
  280.4 3.5 dynamic-slice_reduce_fusion.2
  392.2 3.5 dynamic-slice_reduce_fusion.2
  429.5 3.5 dynamic-slice_reduce_fusion.2
  441.9 3.5 dynamic-slice_reduce_fusion.2
  454.4 3.5 dynamic-slice_reduce_fusion.2
  462.4 50.6 %copy.73 = bf16[32,4,2,16384]{0,1,2,3:T(4,128)(2,1)} copy(bf16[32,4,2,16384]{3,2,1,0:T(2,128)(2,1)} %get-tuple-element.188) | data formatting | bytes 16777216 | tf_op jit(solution)/shard_map/while | solution.py:92
  513.0 23.3 %bitcast_bitcast_fusion = bf16[16384,1,2,4,32]{4,3,2,1,0:T(4,128)(2,1)} fusion(bf16[32,4,2,16384]{0,1,2,3:T(4,128)(2,1)} %copy.73), kind=kLoop, calls=%fused_computation.66 | loop fusion | bytes 16777216
  536.4 35.0 %reshape.221 = bf16[16,2,131072]{2,1,0:T(2,128)(2,1)} reshape(bf16[16384,1,2,4,32]{4,3,2,1,0:T(4,128)(2,1)} %bitcast_bitcast_fusion) | data formatting | bytes 16777216
  571.4 188.9 %all_to_all.30 = bf16[16,2,131072]{2,1,0:T(2,128)(2,1)} all-to-all(bf16[16,2,131072]{2,1,0:T(2,128)(2,1)} %reshape.221), channel_id=1, replica_groups=mesh['stn'=2,'tm'=8,'cores'=2] {'stn','tm'}, dimensions={0} | all-to-all | bytes 16777216 | tf_op jit(solution)/shard_map/all_to_all | solution.py:100
  760.3 22.8 %reshape.222 = bf16[16384,1,2,4,32]{4,3,2,1,0:T(4,128)(2,1)} reshape(bf16[16,2,131072]{2,1,0:T(2,128)(2,1)} %all_to_all.30) | data formatting | bytes 16777216
  783.1 45.2 %copy.89 = bf16[1,32,4,2,16,1024]{5,1,3,2,4,0:T(8,128)(2,1)} copy(bf16[1,32,4,2,16,1024]{1,2,3,5,4,0:T(4,128)(2,1)} %bitcast.102) | data formatting | bytes 16777216 | tf_op jit(solution)/shard_map/all_to_all | solution.py:100
  828.3 8.5 copy.76
  836.8 14.4 %reshape_reshape.3 = bf16[64,32,2,2,512]{4,3,0,2,1:T(2,128)(2,1)} reshape(bf16[2,32,8,4,2,1024]{5,1,0,4,3,2:T(8,128)(2,1)} %copy.76) | data formatting | bytes 16777216 | tf_op jit(solution)/shard_map/reshape;reshape | solution.py:107
  851.2 8.6 copy.77
  859.8 6.9 all-to-all-start.1
  866.8 145.2 %psum.7 = f32[32,128]{1,0:T(8,128)S(1)} all-reduce(f32[32,128]{1,0:T(8,128)S(1)} %get-tuple-element.189), channel_id=1, replica_groups=mesh['stn'=2,'tm'=8,'cores'=2] {'tm','cores'}, use_global_device_ids=true, to_apply=%region_3.4 | all-reduce | flops 4096 | bytes 32768 | tf_op jit(solution)/shard_map/psum | solution.py:95
  1012.6 11.9 %copy.80 = bf16[512,64,128]{2,1,0:T(8,128)(2,1)} copy(bf16[512,64,128]{0,2,1:T(8,128)(2,1)} %bitcast.15) | data formatting | bytes 16777216 | tf_op jit(solution)/shard_map/reshape | solution.py:111
  1024.5 18.8 %fusion.35 = f32[512,128,128]{2,1,0:T(8,128)} fusion(bf16[512,64,128]{2,1,0:T(8,128)(2,1)} %copy.80), kind=kOutput, calls=%fused_computation.67 | convolution fusion | flops 1073741824 | bytes 41943040 | tf_op jit(solution)/shard_map/cta,ctb->cab/dot_general | solution.py:62
  1043.3 34.2 %slice_add_fusion = (f32[512,64,64]{2,1,0:T(8,128)}, f32[512,64,64]{2,1,0:T(8,128)}) fusion(f32[512,128,128]{2,1,0:T(8,128)} %fusion.35), kind=kLoop, calls=%fused_computation.34 | loop fusion | flops 4194304 | bytes 50331648 | tf_op jit(solution)/shard_map/add | solution.py:68
  1077.5 12.7 %copy.82 = f32[512,64,64]{0,2,1:T(8,128)} copy(f32[512,64,64]{2,1,0:T(8,128)} %get-tuple-element.279) | data formatting | bytes 16777216 | tf_op jit(solution)/shard_map/add | solution.py:68
  1090.2 12.7 %copy.83 = f32[512,64,64]{0,2,1:T(8,128)} copy(f32[512,64,64]{2,1,0:T(8,128)} %get-tuple-element.280) | data formatting | bytes 16777216 | tf_op jit(solution)/shard_map/sub | solution.py:69
  1103.0 11.6 %maximum_multiply_fusion = f32[512,8192]{0,1:T(8,128)} fusion(f32[512,4096]{0,1:T(8,128)} %bitcast.105, f32[512,4096]{0,1:T(8,128)} %bitcast.104), kind=kLoop, calls=%fused_computation.35 | loop fusion | flops 8388608 | bytes 33554432 | tf_op jit(solution)/shard_map/mul | solution.py:113
  1114.5 17.4 %copy.84 = f32[512,8192]{1,0:T(8,128)} copy(f32[512,8192]{0,1:T(8,128)} %maximum_multiply_fusion) | data formatting | bytes 33554432
  (453 shorter events, 284.7 us)
Async XLA Ops:
  3.7 50.7 %collective-permute-start = (bf16[32,32768]{1,0:T(8,128)(2,1)}, bf16[32,32768]{1,0:T(8,128)(2,1)S(1)}, u32[]{:S(2)}, u32[]{:S(2)}) collective-permute-start(bf16[32,32768]{1,0:T(8,128)(2,1)} %slice.31), channel_id=1, source_target_pairs={{1,0},{2,1},{3,2},{4,3},{5,4},{6,5},{7,6},{8,7},{9,8},{10,9},{11,1... | collective-permute-start | bytes 6291464 | tf_op jit(solution)/shard_map/ppermute | solution.py:19
  6.5 58.3 %copy-start = (s32[32]{0:T(128)S(1)}, s32[32]{0:T(128)}, u32[]{:S(2)}) copy-start(s32[32]{0:T(128)} %param.7) | copy-start | bytes 388
  6.5 58.3 %copy-start.1 = (s32[32]{0:T(128)S(1)}, s32[32]{0:T(128)}, u32[]{:S(2)}) copy-start(s32[32]{0:T(128)} %param.8) | copy-start | bytes 388
  859.8 152.7 %all-to-all-start.1 = ((bf16[64,32,2,2,512]{4,0,2,1,3:T(8,128)(2,1)}), bf16[64,32,2,2,512]{4,0,2,1,3:T(8,128)(2,1)}, u32[]{:S(2)}, u32[]{:S(2)}) async-start(bf16[64,32,2,2,512]{4,0,2,1,3:T(8,128)(2,1)} %copy.77), calls=%async_computation.1 | async-start | bytes 16777216 | tf_op jit(solution)/shard_map/all_to_all | solution.py:108
where the time goes:
time: 1140 us; the launch traced here: 1130 us
  local copies, waits for them, and re-layouts  476 us (42%)
  blocking collectives  334 us (29%)
  matrix products  105 us (9%)
  loops' own time  81.1 us (7%)
  other arithmetic  79.8 us (7%)
  waiting for transfers between devices  47.9 us (4%)
    all_to_all x1, blocking collectives, shards(): lax.all_to_all(spectra[None], ('stn', 'tm'), split_axis=4, concat_axis=0,...  189 us
    psum x1, blocking collectives, shards(): phase_cal = lax.psum(tone_picks, ('tm', 'cores')) * norm_scale  145 us
    dynamic_slice x32, local copies, waits for them, and re-layouts, station(): window = lax.dynamic_slice_in_dim(stream, shift_by, stretch)  111 us
    unnamed x8, local copies, waits for them, and re-layouts  98.6 us
    another operation x1, loops' own time, shards(): spectra, tone_picks = lax.map(station, (extended, delays, valid, tone_chan))  81.1 us
    dot_general x32, matrix products, station(): jnp.dot(totals, selector, precision=lax.Precision.HIGHEST, preferred_elem...  66.6 us
    while x1, local copies, waits for them, and re-layouts, shards(): spectra, tone_picks = lax.map(station, (extended, delays, valid, tone_chan))  50.6 us
    ppermute x1, waiting for transfers between devices, passed_along(): return lax.ppermute(block, axis, route)  47.9 us
  transfers between devices with their start and end apart: 2, of which 1 were waited for; matrix products, arithmetic and copies ran while one was open for 0% of the time, Pallas kernels for 0%

commit v1 on v0

--- a/solution.py
+++ b/solution.py
@@ -3,6 +3,8 @@
 import jax
 import jax.numpy as jnp
 from jax import lax
+from jax.experimental import pallas as pl
+from jax.experimental.pallas import tpu as pltpu
 from jax.sharding import PartitionSpec as P
 
 S = 64
@@ -113,9 +115,298 @@
     return (partial_value * norm_scale, phase_cal)
 
 
+LANES = 128
+VMEM_LIMIT = 56 * 1024 * 1024
+
+
+def fast_tables():
+    section_one, twist_cos, twist_sin, section_two = make_tables()
+    first = section_one.reshape(2 * FA, FA)
+    last = jnp.concatenate([section_two[0, :, 0], section_two[1, :, 0]], axis=0).T
+    return first, twist_cos, twist_sin, last
+
+
+def channelize_kernel(delay_ref, valid_ref, main_ref, next_ref, one_ref, cos_ref, sin_ref, two_ref,
+                      out_ref, stream, twist_re, twist_im, turned):
+    s = pl.program_id(0)
+    stations = pl.num_programs(0)
+    rows = 2 * FA
+    stream[0:rows, :] = main_ref[0].astype(jnp.float32)
+    stream[rows : rows + FA, :] = next_ref[0].astype(jnp.float32)
+    delay = delay_ref[s]
+    whole = delay // LANES
+    part = delay % LANES
+    lane = lax.broadcasted_iota(jnp.int32, (rows, LANES), 1)
+    here = stream[pl.ds(whole, rows), :]
+    after = stream[pl.ds(whole + 1, rows), :]
+    mixed = jnp.where(lane < part, after, here)
+    shifted = pltpu.roll(mixed, (LANES - part) % LANES, 1).astype(jnp.bfloat16)
+    both = jnp.concatenate([shifted[:FA], shifted[FA:]], axis=1)
+    section = jnp.dot(one_ref[...], both, preferred_element_type=jnp.float32)
+    usable = valid_ref[s].astype(jnp.float32)
+    cosine = cos_ref[...] * usable
+    sine = sin_ref[...] * usable
+    for t in range(2):
+        re = section[:FA, t * LANES : (t + 1) * LANES]
+        im = section[FA:, t * LANES : (t + 1) * LANES]
+        twist_re[pl.ds(t * 32 + s, FA, stride=64), :] = re * cosine + im * sine
+        twist_im[pl.ds(t * 32 + s, FA, stride=64), :] = im * cosine - re * sine
+
+    @pl.when(s == stations - 1)
+    def _():
+        def second(k, carry):
+            at = pl.multiple_of(k * 64, 64)
+            re = twist_re[pl.ds(at, 64), :].astype(jnp.bfloat16)
+            im = twist_im[pl.ds(at, 64), :].astype(jnp.bfloat16)
+            right = jnp.concatenate(
+                [jnp.concatenate([re, im], axis=1), jnp.concatenate([im, -re], axis=1)], axis=0
+            )
+            product = lax.dot_general(
+                two_ref[...], right, (((1,), (1,)), ((), ())), preferred_element_type=jnp.float32
+            )
+            turned[pl.ds(k, FB // 2, stride=FA), :] = product
+            return carry
+
+        lax.fori_loop(0, FA, second, 0, unroll=8)
+
+        def write(q, carry):
+            at = pl.multiple_of(q * FA, FA)
+            out_ref[q] = turned[pl.ds(at, FA), :].astype(jnp.bfloat16)
+            return carry
+
+        lax.fori_loop(0, FB // 2, write, 0, unroll=2)
+
+
+def channelize_pair(pair, blocks, following, delays, valid, tables):
+    first, twist_cos, twist_sin, last = tables
+    source, next_at = following
+    whole = lambda shape: pl.BlockSpec(shape, lambda s, *_: (0,) * len(shape))
+    return pl.pallas_call(
+        channelize_kernel,
+        out_shape=jax.ShapeDtypeStruct((FB // 2, FA, LANES), jnp.bfloat16),
+        grid_spec=pltpu.PrefetchScalarGridSpec(
+            num_scalar_prefetch=2,
+            grid=(blocks.shape[0],),
+            in_specs=[
+                pl.BlockSpec((1, 2 * FA, LANES), lambda s, *_: (s, pair, 0)),
+                pl.BlockSpec((1, FA, LANES), lambda s, *_: (s, next_at, 0)),
+                whole((2 * FA, FA)),
+                whole((FA, FB)),
+                whole((FA, FB)),
+                whole((FB // 2, 2 * FB)),
+            ],
+            out_specs=whole((FB // 2, FA, LANES)),
+            scratch_shapes=[
+                pltpu.VMEM((3 * FA + 8, LANES), jnp.float32),
+                pltpu.VMEM((FA * 64, LANES), jnp.float32),
+                pltpu.VMEM((FA * 64, LANES), jnp.float32),
+                pltpu.VMEM((FA * 64, LANES), jnp.float32),
+            ],
+        ),
+        compiler_params=pltpu.CompilerParams(vmem_limit_bytes=VMEM_LIMIT),
+        cost_estimate=pl.CostEstimate(
+            flops=3 * 2 * 64 * 256 * 256 * 256, bytes_accessed=10 * 2**20, transcendentals=0
+        ),
+    )(delays, valid, blocks, source, first, twist_cos, twist_sin, last)
+
+
+def exchange_kernel(sizes, zero_ref, one_ref, got_ref, local_sem, send_sem, recv_sem):
+    n_stn, n_tm, n_cores = sizes
+    n = n_stn * n_tm * n_cores
+    me = (lax.axis_index("stn") * n_tm + lax.axis_index("tm")) * n_cores + lax.axis_index("cores")
+
+    def place(device):
+        return (device // (n_tm * n_cores), (device // n_cores) % n_tm, device % n_cores)
+
+    barrier = pltpu.get_barrier_semaphore()
+
+    def greet(k, carry):
+        pl.semaphore_signal(
+            barrier, inc=1, device_id=place((me + k) % n), device_id_type=pl.DeviceIdType.MESH
+        )
+        return carry
+
+    lax.fori_loop(1, n, greet, 0)
+    pl.semaphore_wait(barrier, n - 1)
+    sources = (zero_ref, one_ref)
+
+    def copy(pair, k):
+        to = (me + k) % n
+        return pltpu.make_async_remote_copy(
+            src_ref=sources[pair].at[pl.ds(to * 2, 2)],
+            dst_ref=got_ref.at[pair, me],
+            send_sem=send_sem.at[pair, k],
+            recv_sem=recv_sem.at[pair, k],
+            device_id=place(to),
+            device_id_type=pl.DeviceIdType.MESH,
+        )
+
+    for pair in range(2):
+        lax.fori_loop(1, n, lambda k, carry, pair=pair: (copy(pair, k).start(), carry)[1], 0)
+    own = [
+        pltpu.make_async_copy(
+            sources[pair].at[pl.ds(me * 2, 2)], got_ref.at[pair, me], local_sem.at[pair]
+        )
+        for pair in range(2)
+    ]
+    for one in own:
+        one.start()
+    for one in own:
+        one.wait()
+    for pair in range(2):
+        lax.fori_loop(1, n, lambda k, carry, pair=pair: (copy(pair, k).wait(), carry)[1], 0)
+
+
+def exchange(zero, one, sizes):
+    n = math.prod(sizes)
+    return pl.pallas_call(
+        lambda *refs: exchange_kernel(sizes, *refs),
+        out_shape=jax.ShapeDtypeStruct((2, n, 2, FA, LANES), jnp.bfloat16),
+        in_specs=[pl.BlockSpec(memory_space=pl.ANY)] * 2,
+        out_specs=pl.BlockSpec(memory_space=pl.ANY),
+        scratch_shapes=[
+            pltpu.SemaphoreType.DMA((2,)),
+            pltpu.SemaphoreType.DMA((2, n)),
+            pltpu.SemaphoreType.DMA((2, n)),
+        ],
+        compiler_params=pltpu.CompilerParams(collective_id=0, has_side_effects=True),
+    )(zero, one)
+
+
+CB = 64
+
+
+def tones_kernel(first_ref, tone_ref, got_ref, out_ref, total):
+    step = pl.program_id(0)
+
+    @pl.when(step == 0)
+    def _():
+        out_ref[...] = jnp.zeros_like(out_ref)
+
+    lane = lax.broadcasted_iota(jnp.int32, (CB, LANES), 1)
+    sums = []
+    for y in range(2):
+        acc = jnp.zeros((CB, LANES), jnp.float32)
+        for u in range(2):
+            for j in range(got_ref.shape[2]):
+                acc = acc + got_ref[u, y, j].astype(jnp.float32)
+        sums.append(acc + pltpu.roll(acc, 96, 1))
+    total[...] = jnp.where(lane % 64 < 32, sums[0], pltpu.roll(sums[1], 32, 1))
+    start = first_ref[0] + step * CB
+    picked = out_ref[...]
+    for c in range(CB):
+        picked = picked + jnp.where(tone_ref[...] == start + c, total[c : c + 1, :], 0.0)
+    out_ref[...] = picked
+
+
+def tones(got, tone_lanes, first_channel):
+    _, n_stn, n_time, channels, _ = got.shape
+    return pl.pallas_call(
+        tones_kernel,
+        out_shape=jax.ShapeDtypeStruct((NTONE, LANES), jnp.float32),
+        grid_spec=pltpu.PrefetchScalarGridSpec(
+            num_scalar_prefetch=1,
+            grid=(channels // CB,),
+            in_specs=[
+                pl.BlockSpec((NTONE, LANES), lambda i, *_: (0, 0)),
+                pl.BlockSpec((2, n_stn, n_time, CB, LANES), lambda i, *_: (0, 0, 0, i, 0)),
+            ],
+            out_specs=pl.BlockSpec((NTONE, LANES), lambda i, *_: (0, 0)),
+            scratch_shapes=[pltpu.VMEM((CB, LANES), jnp.float32)],
+        ),
+        compiler_params=pltpu.CompilerParams(vmem_limit_bytes=VMEM_LIMIT),
+    )(first_channel, tone_lanes, got)
+
+
+def correlate_kernel(scale, got_ref, out_ref, matrix, power, turned):
+    lane = lax.broadcasted_iota(jnp.int32, (CB, LANES), 1)
+    low = lane % 64 < 32
+    n_time = got_ref.shape[2]
+    rows = 4 * n_time
+    for u in range(2):
+        for j in range(n_time):
+            y0 = got_ref[u, 0, j].astype(jnp.float32)
+            y1 = got_ref[u, 1, j].astype(jnp.float32)
+            t = (u * n_time + j) * 2
+            matrix[pl.ds(t, CB, stride=rows), :] = jnp.where(low, y0, pltpu.roll(y1, 32, 1))
+            matrix[pl.ds(t + 1, CB, stride=rows), :] = jnp.where(low, pltpu.roll(y0, 96, 1), y1)
+    left = lax.broadcasted_iota(jnp.int32, (S, LANES), 1) < 64
+    left_half = lax.broadcasted_iota(jnp.int32, (S // 2, LANES), 1) < 64
+
+    def channel(c, carry):
+        at = pl.multiple_of(c * rows, rows)
+        values = matrix[pl.ds(at, rows), :].astype(jnp.bfloat16)
+        gram = lax.dot_general(
+            values, values, (((0,), (0,)), ((), ())), preferred_element_type=jnp.float32
+        )
+        upper = gram[:S] * scale
+        lower = pltpu.roll(gram[S:] * scale, 64, 1)
+        slot = pl.multiple_of((c % 8) * S, S)
+        power[pl.ds(slot, S), :] = jnp.where(left, upper + lower, lower - upper)
+        even = power[pl.ds(slot, S // 2, stride=2), :]
+        odd = power[pl.ds(slot + 1, S // 2, stride=2), :]
+        turned[pl.ds(c, S // 2, stride=CB), :] = jnp.where(left_half, even, pltpu.roll(odd, 64, 1))
+        turned[pl.ds(S // 2 * CB + c, S // 2, stride=CB), :] = jnp.where(
+            left_half, pltpu.roll(even, 64, 1), odd
+        )
+        return carry
+
+    lax.fori_loop(0, CB, channel, 0, unroll=8)
+    for tile in range(S):
+        out_ref[:, tile * LANES : (tile + 1) * LANES] = turned[tile * CB : (tile + 1) * CB, :]
+
+
+def correlate(got, scale):
+    _, n_stn, n_time, channels, _ = got.shape
+    return pl.pallas_call(
+        lambda *refs: correlate_kernel(scale, *refs),
+        out_shape=jax.ShapeDtypeStruct((channels, 2 * S * S), jnp.float32),
+        grid=(channels // CB,),
+        in_specs=[pl.BlockSpec((2, n_stn, n_time, CB, LANES), lambda i: (0, 0, 0, i, 0))],
+        out_specs=pl.BlockSpec((CB, 2 * S * S), lambda i: (i, 0)),
+        scratch_shapes=[
+            pltpu.VMEM((CB * 4 * n_time, LANES), jnp.float32),
+            pltpu.VMEM((8 * S, LANES), jnp.float32),
+            pltpu.VMEM((S * CB, LANES), jnp.float32),
+        ],
+        compiler_params=pltpu.CompilerParams(vmem_limit_bytes=VMEM_LIMIT),
+        cost_estimate=pl.CostEstimate(
+            flops=2 * channels * 64 * 128 * 128, bytes_accessed=26 * 2**20, transcendentals=0
+        ),
+    )(got)
+
+
+def fast_shards(samples, delays, valid, tone_chan):
+    tables = fast_tables()
+    sizes = tuple(lax.axis_size(name) for name in ("stn", "tm", "cores"))
+    n_stn, n_tm, n_cores = sizes
+    stations, stretch = samples.shape
+    trailing = passed_along(samples[:, :MAXD], ("tm", "cores"), -1)
+    blocks = samples.reshape(stations, stretch // LANES, LANES)
+    zero = channelize_pair(0, blocks, (blocks, 2), delays, valid, tables)
+    halo = trailing.reshape(stations, MAXD // LANES, LANES)
+    one = channelize_pair(1, blocks, (halo, 0), delays, valid, tables)
+    channels = NCH // (n_stn * n_tm * n_cores)
+    got = exchange(zero, one, sizes).reshape(2, n_stn, n_tm * n_cores, channels, LANES)
+    scale = 1.0 / math.sqrt(stretch // (FA * FB) * n_tm * n_cores)
+    me = (lax.axis_index("stn") * n_tm + lax.axis_index("tm")) * n_cores + lax.axis_index("cores")
+    everyone = lax.all_gather(tone_chan, "stn", axis=0, tiled=True)
+    tone_lanes = jnp.concatenate([everyone.T, everyone.T], axis=1)
+    picks = tones(got, tone_lanes, (me * channels).astype(jnp.int32)[None])
+    picks = lax.psum(picks, ("stn", "tm", "cores")) * scale
+    visibility = correlate(got, scale)
+    mine = lax.dynamic_slice_in_dim(
+        picks.reshape(NTONE, 2, S), lax.axis_index("stn") * stations, stations, axis=2
+    )
+    phase_cal = jnp.transpose(mine, (2, 1, 0)).reshape(stations, 2 * NTONE)
+    return (visibility, phase_cal)
+
+
 def solution(mesh):
+    sizes = mesh.shape
+    body = fast_shards if sizes["stn"] == 2 and math.prod(sizes.values()) == 32 else shards
     return jax.shard_map(
-        shards,
+        body,
         mesh=mesh,
         in_specs=(P("stn", ("tm", "cores")), P("stn"), P("stn"), P("stn", None)),
         out_specs=(P(("stn", "tm", "cores"), None), P("stn", None)),

time: 1140 us -> 426 us (0.37)
  local copies, waits for them, and re-layouts: 476 us -> 14.7 us
  Pallas kernels: 0 us -> 340 us
  blocking collectives: 334 us -> 62.9 us
  matrix products: 105 us -> 0 us
  loops' own time: 81.1 us -> 0 us
  other arithmetic: 79.8 us -> 4.82 us
  waiting for transfers between devices: 47.9 us -> 0.01 us
    pallas_call x0 -> x5, Pallas kernels: none -> 340 us  [the longest x1 183 us: exchange(): pl.pallas_call(lambda *refs: exchange_kernel(sizes, *refs), out_shape=jax...]
    all_to_all x1 -> x0, blocking collectives: 189 us -> none  [shards(): lax.all_to_all(spectra[None], ('stn', 'tm'), split_axis=4, concat_axis=0,...]
    dynamic_slice x96 -> x0, local copies, waits for them, and re-layouts: 149 us -> none  [the longest x32 111 us: station(): window = lax.dynamic_slice_in_dim(stream, shift_by, stretch)]
    dot_general x97 -> x0, matrix products: 105 us -> none  [the longest x32 66.6 us: station(): jnp.dot(totals, selector, precision=lax.Precision.HIGHEST, preferred_elem...]
    unnamed x8 -> x4, local copies, waits for them, and re-layouts: 98.6 us -> 10.6 us
    psum x1, blocking collectives: 145 us -> 57.6 us  [fast_shards(): picks = lax.psum(picks, ('stn', 'tm', 'cores')) * scale]
    another operation x1 -> x0, loops' own time: 81.1 us -> none  [shards(): spectra, tone_picks = lax.map(station, (extended, delays, valid, tone_chan))]
    while x33 -> x0, local copies, waits for them, and re-layouts: 53.9 us -> none  [the longest x1 50.6 us: shards(): spectra, tone_picks = lax.map(station, (extended, delays, valid, tone_chan))]
  transfers between devices with their start and end apart: 2 -> 1, of which waited for: 1 -> 0; matrix products, arithmetic and copies ran while one was open for 0% -> 3% of each run, Pallas kernels for 0% -> 10%
where the time goes in v1:
time: 426 us; the launch traced here: 424 us
  Pallas kernels  340 us (80%)
  blocking collectives  62.9 us (15%)
  local copies, waits for them, and re-layouts  14.7 us (3%)
  other arithmetic  4.82 us (1%)
    pallas_call x1, Pallas kernels, exchange(): pl.pallas_call(lambda *refs: exchange_kernel(sizes, *refs), out_shape=jax...  183 us
    pallas_call x2, Pallas kernels, channelize_pair(): pl.pallas_call(channelize_kernel, out_shape=jax.ShapeDtypeStruct((FB // 2...  88.2 us
    pallas_call x1, Pallas kernels, correlate(): pl.pallas_call(lambda *refs: correlate_kernel(scale, *refs), out_shape=ja...  61.4 us
    psum x1, blocking collectives, fast_shards(): picks = lax.psum(picks, ('stn', 'tm', 'cores')) * scale  57.6 us
    unnamed x4, local copies, waits for them, and re-layouts  10.6 us
  transfers between devices with their start and end apart: 1, of which 0 were waited for; matrix products, arithmetic and copies ran while one was open for 3% of the time, Pallas kernels for 10%

profile of v1, /device:TPU:0, one launch (start us, length us, event | category | flops | bytes accessed | tf_op | source)
XLA Modules:
  0.0 424.4 jit_solution(12906421904295990050)
XLA Ops:
  0.6 0.0 copy-start
  0.6 3.1 slice.13
  3.7 1.3 collective-permute-start
  5.0 0.0 copy-done
  5.0 5.3 %all_gather.3 = s32[64,64]{1,0:T(8,128)S(1)} all-gather(s32[32,64]{1,0:T(8,128)S(1)} %copy-done), channel_id=1, replica_groups=mesh['stn'=2,'tm'=8,'cores'=2] {'stn'}, dimensions={0}, use_global_device_ids=true | all-gather | bytes 24576 | tf_op jit(solution)/shard_map/all_gather | solution.py:393
  10.3 0.1 copy.8
  10.4 8.8 %copy.10 = bf16[4,8,1024,128]{3,2,1,0:T(8,128)(2,1)} copy(bf16[4,8,1024,128]{3,1,2,0:T(8,128)(2,1)} %bitcast.22) | data formatting | bytes 16777216
  19.2 0.1 fusion.19
  19.3 0.1 cosine_convert_fusion.1
  19.5 0.1 negate_convert_fusion.1
  19.6 0.7 pad_add_fusion.tone_ref
  20.3 0.6 maximum_bitcast_fusion.2.two_ref
  20.9 1.2 sine_multiply_fusion
  22.2 1.1 negate_convert_fusion
  23.3 0.7 pad_maximum_fusion
  24.0 44.1 %shard_map.59.refs_0_ = bf16[64,256,128]{2,1,0:T(8,128)(2,1)} custom-call(s32[32]{0:T(128)} %delay_ref.3, s32[32]{0:T(128)} %valid_ref.3, bf16[32,1024,128]{2,1,0:T(8,128)(2,1)} %bitcast.23, bf16[32,1024,128]{2,1,0:T(8,128)(2,1)} %bitcast.24, bf16[512,256]{1,0:T(8,128)(2,1)} %bitcast.28, f32[256,128]{1,0:T(8,128)} %get-tuple-element.9.cos_ref, ...), custom_call_target="tpu_custom_call" | custom-call | flops 6442450944 | bytes 10485760 | tf_op jit(solution)/shard_map/pallas_call | solution.py:184
  68.1 0.0 collective-permute-done
  68.1 1.8 copy.11
  69.9 44.1 %shard_map.60.refs_1_ = bf16[64,256,128]{2,1,0:T(8,128)(2,1)} custom-call(s32[32]{0:T(128)} %delay_ref.3, s32[32]{0:T(128)} %valid_ref.3, bf16[32,1024,128]{2,1,0:T(8,128)(2,1)} %bitcast.25, bf16[32,256,128]{2,1,0:T(8,128)(2,1)} %bitcast.27, bf16[512,256]{1,0:T(8,128)(2,1)} %bitcast.29, f32[256,128]{1,0:T(8,128)} %get-tuple-element.9.cos_ref, ...), custom_call_target="tpu_custom_call" | custom-call | flops 6442450944 | bytes 10485760 | tf_op jit(solution)/shard_map/pallas_call | solution.py:184
  114.1 182.5 %shard_map.61 = bf16[2,32,2,256,128]{4,3,2,1,0:T(8,128)(2,1)} custom-call(bf16[64,256,128]{2,1,0:T(8,128)(2,1)} %shard_map.59.refs_0_, bf16[64,256,128]{2,1,0:T(8,128)(2,1)} %shard_map.60.refs_1_), custom_call_target="tpu_custom_call" | custom-call | tf_op jit(solution)/shard_map/pallas_call | solution.py:262
  296.6 61.4 %shard_map.62 = f32[512,8192]{1,0:T(8,128)} custom-call(bf16[2,2,16,512,128]{4,3,2,1,0:T(8,128)(2,1)} %bitcast.20), custom_call_target="tpu_custom_call" | custom-call | flops 1073741824 | bytes 27262976 | tf_op jit(solution)/shard_map/pallas_call | solution.py:361
  358.0 7.8 %shard_map.63 = f32[64,128]{1,0:T(8,128)} custom-call(s32[1]{0:T(128)} %bitcast.7.first_ref, s32[64,128]{1,0:T(8,128)} %pad_add_fusion.tone_ref, bf16[2,2,16,512,128]{4,3,2,1,0:T(8,128)(2,1)} %bitcast.21), custom_call_target="tpu_custom_call" | custom-call | tf_op jit(solution)/shard_map/pallas_call | solution.py:304
  365.8 57.6 %psum.7 = f32[64,128]{1,0:T(8,128)S(1)} all-reduce(f32[64,128]{1,0:T(8,128)} %shard_map.63), channel_id=1, replica_groups=mesh['stn'=2,'tm'=8,'cores'=2] {'stn','tm','cores'}, use_global_device_ids=true, to_apply=%region_0.1 | all-reduce | flops 8192 | bytes 65536 | tf_op jit(solution)/shard_map/psum | solution.py:396
  423.4 0.1 reshape.171
  423.5 0.1 dynamic-slice_bitcast_fusion
  423.6 0.1 copy.9
  423.7 0.7 reshape.172
  (3 shorter events, 0.0 us)
Async XLA Ops:
  0.6 4.4 %copy-start = (s32[32,64]{1,0:T(8,128)S(1)}, s32[32,64]{1,0:T(8,128)}, u32[]{:S(2)}) copy-start(s32[32,64]{1,0:T(8,128)} %param.7) | copy-start | bytes 24580
  3.7 64.4 %collective-permute-start = (bf16[32,32768]{1,0:T(8,128)(2,1)}, bf16[32,32768]{1,0:T(8,128)(2,1)S(1)}, u32[]{:S(2)}, u32[]{:S(2)}) collective-permute-start(bf16[32,32768]{1,0:T(8,128)(2,1)} %slice.13), channel_id=1, source_target_pairs={{1,0},{2,1},{3,2},{4,3},{5,4},{6,5},{7,6},{8,7},{9,8},{10,9},{11,1... | collective-permute-start | bytes 6291464 | tf_op jit(solution)/shard_map/ppermute | solution.py:21
